TPU v7x, 32 devices: a whole 2x2x4 slice. The times are simulated.
32 devices in a mesh: groups: 2 (over y), dp: 8 (over z, x), shard: 2 (over core).
Axes of the slice: x: 2, y: 2, z: 4, core: 2. Of those that a mesh axis runs over, the one named last changes fastest.
Arguments:
- projected: bfloat16 [8192, 4096], P(('groups', 'dp', 'shard')), parts along dimension 0, may hold values from -6 to 6
- grad_gated: bfloat16 [8192, 1024], P(('groups', 'dp', 'shard')), parts along dimension 0, may hold values from -6 to 6
- lengths: int32 [170], P('groups'), parts along dimension 0, may hold values from 1 to 96, 4096 in all
Outputs:
- grad_projected: bfloat16 [8192, 4096], P(('groups', 'dp', 'shard')), parts along dimension 0
There are 2 independent parts, one for each index of `groups`. A program takes and returns all parts, laid end to end along the dimension named above; each array names one. Nothing has to cross between parts.
Inputs may be any that keep to these rules, and one draw needn't show every extreme that they name: The lengths sum to 4096 and the longest is exactly 96.
All inputs are finite; a program needn't handle non-finite values.
Results may differ from a plain program's by a relative error of at most 0.0055.
Values may be sent and summed in bfloat16 or wider, within the bound.
A program may use at most 64 MiB of HBM per device.

v0:
```python
import functools

import jax
import jax.numpy as jnp
from jax import lax
from jax.experimental import pallas as pl
from jax.experimental.pallas import tpu as pltpu
from jax.sharding import PartitionSpec as P

HEADS = 16
MAXLEN = 96
BLOCK = 64
KEYS = BLOCK + MAXLEN
QUAD = 4
CHUNK = 32
MESH = pl.DeviceIdType.MESH


def dot(a, b, ca, cb):
    return lax.dot_general(a, b, (((ca,), (cb,)), ((), ())), preferred_element_type=jnp.float32)


def kernel(
    n_dp, n_shard,
    proj, grad, lengths, out,
    kv, q, u, dy, mixed, gm, weights, slopes, acc, ones, sixteenths, masks, result,
    outgoing, returned,
    load_sem, store_sem, halo_send, halo_recv, back_send, back_recv,
):
    rows, width = q.shape
    quad = QUAD * (width // HEADS)
    quads = width // quad
    blocks = rows // BLOCK
    tail = rows - MAXLEN
    half = blocks // 2

    me = lax.axis_index("dp") * n_shard + lax.axis_index("shard")
    last = n_dp * n_shard - 1
    has_prev, has_next = me > 0, me < last

    def device(index):
        return {"dp": index // n_shard, "shard": index % n_shard}

    barrier = pltpu.get_barrier_semaphore()

    @pl.when(has_prev)
    def _():
        pl.semaphore_signal(barrier, inc=1, device_id=device(me - 1), device_id_type=MESH)

    @pl.when(has_next)
    def _():
        pl.semaphore_signal(barrier, inc=1, device_id=device(me + 1), device_id_type=MESH)

    def load(i, source, target):
        copy = pltpu.make_async_copy(source, target, load_sem.at[i])
        copy.start()
        return copy

    loads = [
        load(0, proj.at[:, pl.ds(width, 2 * width)], kv.at[pl.ds(MAXLEN, rows), :]),
        load(1, proj.at[:, pl.ds(0, width)], q),
        load(2, proj.at[:, pl.ds(3 * width, width)], u),
        load(3, grad, dy),
    ]

    pl.semaphore_wait(barrier, jnp.where(has_prev, 1, 0) + jnp.where(has_next, 1, 0))

    halo = pltpu.make_async_remote_copy(
        src_ref=proj.at[pl.ds(tail, MAXLEN), pl.ds(width, 2 * width)],
        dst_ref=kv.at[pl.ds(0, MAXLEN), :],
        send_sem=halo_send,
        recv_sem=halo_recv,
        device_id=device(jnp.where(has_next, me + 1, me - 1)),
        device_id_type=MESH,
    )

    @pl.when(has_next)
    def _():
        halo.start()

    @pl.when(jnp.logical_not(has_prev))
    def _():
        kv[pl.ds(0, MAXLEN), :] = jnp.zeros((MAXLEN, 2 * width), kv.dtype)

    @pl.when(jnp.logical_not(has_next))
    def _():
        returned[...] = jnp.zeros_like(returned)

    def backs(c):
        return pltpu.make_async_remote_copy(
            src_ref=outgoing.at[c],
            dst_ref=returned.at[c],
            send_sem=back_send.at[c],
            recv_sem=back_recv.at[c],
            device_id=device(jnp.where(has_prev, me - 1, me + 1)),
            device_id_type=MESH,
        )

    base = (me * rows).astype(jnp.float32)
    lane = (lax.broadcasted_iota(jnp.int32, (1, quad), 1) % BLOCK).astype(jnp.float32)
    positions = [base + float(b * BLOCK) + lane for b in range(blocks)]
    starts = [jnp.zeros((1, quad), jnp.float32) for _ in range(blocks)]
    carry = jnp.zeros((1, 1), jnp.float32)
    count = lengths.shape[1]
    for first in range(0, count, 128):
        span = min(128, count - first)
        part = lengths[:, first : first + span].astype(jnp.float32)
        upto = lax.broadcasted_iota(jnp.int32, (span, span), 1) <= lax.broadcasted_iota(
            jnp.int32, (span, span), 0
        )
        ends = carry + jnp.sum(jnp.where(upto, part, 0.0), axis=1, keepdims=True)
        carry = carry + jnp.sum(part, axis=1, keepdims=True)
        for b in range(blocks):
            reached = jnp.max(jnp.where(ends <= positions[b], ends, 0.0), axis=0, keepdims=True)
            starts[b] = jnp.maximum(starts[b], reached)
    offset = lax.broadcasted_iota(jnp.int32, (KEYS, quad), 0).astype(jnp.float32)
    for b in range(blocks):
        key = offset + (base + float(b * BLOCK - MAXLEN))
        keep = (starts[b] <= key) & (key <= positions[b])
        masks[b] = jnp.where(keep, 1.0, 0.0)

    own_head = (
        lax.broadcasted_iota(jnp.int32, (quad, quad), 0) // BLOCK
        == lax.broadcasted_iota(jnp.int32, (quad, quad), 1) // (quad // QUAD)
    )
    ones[...] = jnp.where(own_head, 1.0, 0.0).astype(ones.dtype)
    sixteenths[...] = jnp.where(own_head, 0.0625, 0.0).astype(ones.dtype)
    left_head = lax.broadcasted_iota(jnp.int32, (BLOCK, quad // 2), 1) < quad // QUAD

    def stacked(value, head_mask):
        return jnp.concatenate([value] * QUAD, 0) * head_mask[...]

    def block_rows(b):
        return pl.ds(b * BLOCK, BLOCK)

    def columns(c, part=0):
        return pl.ds(part * width + c * quad, quad)

    def per_head(transposed, values):
        halves = []
        for p in range(2):
            lanes = slice(p * quad // 2, (p + 1) * quad // 2)
            both = dot(transposed[:, lanes], values[:, lanes], 0, 0)
            halves.append(jnp.where(left_head, both[:BLOCK], both[BLOCK:]))
        return jnp.concatenate(halves, 1)

    def forward(b, c):
        keys = kv[pl.ds(b * BLOCK, KEYS), columns(c)]
        values = kv[pl.ds(b * BLOCK, KEYS), columns(c, 1)]
        queries = stacked(q[block_rows(b), columns(c)], sixteenths)
        h = dot(keys, queries, 1, 1)
        t = jnp.tanh(h)
        kept = (1.0 + t) * masks[b]
        w = (h * kept).astype(weights.dtype)
        weights[b, c] = w
        slopes[b, c] = kept * (1.0 + h * (1.0 - t))
        mixed[block_rows(b), columns(c)] = per_head(w, values)

    def normalise(b):
        at = block_rows(b)
        m = mixed[at, :]
        centered = m - jnp.mean(m, axis=1, keepdims=True)
        rstd = lax.rsqrt(jnp.mean(centered * centered, axis=1, keepdims=True) + 1e-05)
        normed = centered * rstd
        d = dy[at, :].astype(jnp.float32)
        result[at, pl.ds(3 * width, width)] = (d * normed).astype(result.dtype)
        dn = d * u[at, :].astype(jnp.float32)
        mean_dn = jnp.mean(dn, axis=1, keepdims=True)
        mean_dnn = jnp.mean(dn * normed, axis=1, keepdims=True)
        gm[at, :] = (rstd * (dn - mean_dn - normed * mean_dnn)).astype(gm.dtype)

    written = set()
    left = {}
    for e in range((MAXLEN + rows) // CHUNK):
        users = [b for b in range(blocks) if b * BLOCK <= e * CHUNK < b * BLOCK + KEYS]
        for c in range(quads):
            left[e, c] = len(users)

    def add(b, c, part, value):
        for i in range(KEYS // CHUNK):
            e = b * BLOCK // CHUNK + i
            piece = value[i * CHUNK : (i + 1) * CHUNK]
            at = pl.ds(e * CHUNK, CHUNK)
            if (e, c, part) in written:
                piece = piece + acc[at, columns(c, part)]
            written.add((e, c, part))
            if part:
                left[e, c] -= 1
            remaining = left[e, c] if part else left[e, c] - 1
            row = e * CHUNK - MAXLEN
            if remaining or row >= tail:
                acc[at, columns(c, part)] = piece
            elif row < 0:
                outgoing[c, at, pl.ds(part * quad, quad)] = piece.astype(outgoing.dtype)
            else:
                result[pl.ds(row, CHUNK), columns(c, 1 + part)] = piece.astype(result.dtype)

    def backward(b, c):
        keys = kv[pl.ds(b * BLOCK, KEYS), columns(c)]
        values = kv[pl.ds(b * BLOCK, KEYS), columns(c, 1)]
        queries = stacked(q[block_rows(b), columns(c)], sixteenths)
        grads = stacked(gm[block_rows(b), columns(c)], ones)
        grad_weights = dot(values, grads, 1, 1)
        grad_scores = (grad_weights * slopes[b, c]).astype(jnp.bfloat16)
        add(b, c, 0, dot(grad_scores, queries, 1, 0))
        add(b, c, 1, dot(weights[b, c], grads, 1, 0))
        grad_q = per_head(grad_scores, keys) * 0.0625
        result[block_rows(b), columns(c)] = grad_q.astype(result.dtype)

    stores = []

    def store(row, height, column, span):
        at = (pl.ds(row, height), pl.ds(column, span))
        copy = pltpu.make_async_copy(result.at[at], out.at[at], store_sem.at[len(stores)])
        copy.start()
        stores.append(copy)

    lower, upper = range(half), range(half, blocks)
    split = half * BLOCK

    for copy in loads[:2]:
        copy.wait()
    for c in range(quads):
        for b in upper:
            forward(b, c)
    for copy in loads[2:]:
        copy.wait()
    for b in upper:
        normalise(b)
    store(split, rows - split, 3 * width, width)

    @pl.when(has_prev)
    def _():
        halo.wait_recv()

    for c in range(quads):
        for b in lower:
            forward(b, c)
    for b in lower:
        normalise(b)
    store(0, split, 3 * width, width)
    for c in range(quads):
        for b in lower:
            backward(b, c)

        @pl.when(has_prev)
        def _():
            backs(c).start()

    store(0, split, 0, width)
    for c in range(quads):
        for b in upper:
            backward(b, c)
    store(split, rows - split, 0, width)
    store(0, tail, width, 2 * width)

    for c in range(quads):

        @pl.when(has_next)
        def _():
            backs(c).wait_recv()

        for part in range(2):
            total = acc[pl.ds(rows, MAXLEN), columns(c, part)] + returned[
                c, :, pl.ds(part * quad, quad)
            ].astype(jnp.float32)
            result[pl.ds(tail, MAXLEN), columns(c, 1 + part)] = total.astype(result.dtype)
    store(tail, MAXLEN, width, 2 * width)

    @pl.when(has_next)
    def _():
        halo.wait_send()

    for c in range(quads):

        @pl.when(has_prev)
        def _():
            backs(c).wait_send()

    for copy in stores:
        copy.wait()


def on_device(mesh, projected, grad_gated, lengths):
    rows, width = grad_gated.shape
    quad = QUAD * (width // HEADS)
    quads = width // quad
    blocks = rows // BLOCK
    bf16, f32 = jnp.bfloat16, jnp.float32
    window = rows + MAXLEN
    anywhere = pl.BlockSpec(memory_space=pl.ANY)
    return pl.pallas_call(
        functools.partial(kernel, mesh.shape["dp"], mesh.shape["shard"]),
        out_shape=jax.ShapeDtypeStruct((rows, 4 * width), bf16),
        in_specs=[anywhere, anywhere, pl.BlockSpec(memory_space=pltpu.VMEM)],
        out_specs=anywhere,
        scratch_shapes=[
            pltpu.VMEM((window, 2 * width), bf16),
            pltpu.VMEM((rows, width), bf16),
            pltpu.VMEM((rows, width), bf16),
            pltpu.VMEM((rows, width), bf16),
            pltpu.VMEM((rows, width), f32),
            pltpu.VMEM((rows, width), bf16),
            pltpu.VMEM((blocks, quads, KEYS, quad), bf16),
            pltpu.VMEM((blocks, quads, KEYS, quad), f32),
            pltpu.VMEM((window, 2 * width), f32),
            pltpu.VMEM((quad, quad), bf16),
            pltpu.VMEM((quad, quad), bf16),
            pltpu.VMEM((blocks, KEYS, quad), f32),
            pltpu.VMEM((rows, 4 * width), bf16),
            pltpu.VMEM((quads, MAXLEN, 2 * quad), bf16),
            pltpu.VMEM((quads, MAXLEN, 2 * quad), bf16),
            pltpu.SemaphoreType.DMA((4,)),
            pltpu.SemaphoreType.DMA((6,)),
            pltpu.SemaphoreType.DMA,
            pltpu.SemaphoreType.DMA,
            pltpu.SemaphoreType.DMA((quads,)),
            pltpu.SemaphoreType.DMA((quads,)),
        ],
        compiler_params=pltpu.CompilerParams(
            collective_id=0, has_side_effects=True, vmem_limit_bytes=40 * 1024 * 1024
        ),
        cost_estimate=pl.CostEstimate(
            flops=6 * 2 * rows * KEYS * width * QUAD,
            bytes_accessed=rows * width * 2 * 9,
            transcendentals=rows * KEYS * HEADS,
        ),
    )(projected, grad_gated, lengths.reshape(1, -1))


def solution(mesh):
    in_specs = (P(("groups", "dp", "shard"), None), P(("groups", "dp", "shard"), None), P("groups"))
    out_specs = P(("groups", "dp", "shard"), None)
    return jax.shard_map(
        functools.partial(on_device, mesh),
        mesh=mesh, in_specs=in_specs, out_specs=out_specs, check_vma=False,
    )
```

profile of v0, /device:TPU:1, one launch (start us, length us, event | category | flops | bytes accessed | tf_op | source)
XLA Modules:
  0.0 22.2 jit_solution(5322544940638392411)
XLA Ops:
  0.0 0.0 copy-start
  0.0 1.6 %copy-done = bf16[256,4096]{1,0:T(8,128)(2,1)S(1)} copy-done((bf16[256,4096]{1,0:T(8,128)(2,1)S(1)}, bf16[256,4096]{1,0:T(8,128)(2,1)}, u32[]{:S(2)}) %copy-start) | copy-done | bytes 2097176
  1.6 0.0 copy-start.1
  1.6 1.0 %copy-done.1 = bf16[256,1024]{1,0:T(8,128)(2,1)S(1)} copy-done((bf16[256,1024]{1,0:T(8,128)(2,1)S(1)}, bf16[256,1024]{1,0:T(8,128)(2,1)}, u32[]{:S(2)}) %copy-start.1) | copy-done | bytes 524312
  2.6 0.0 copy-start.2
  2.6 0.7 %copy-done.2 = s32[85]{0:T(128)S(1)} copy-done((s32[85]{0:T(128)S(1)}, s32[85]{0:T(128)}, u32[]{:S(2)}) %copy-start.2) | copy-done | bytes 364
  3.3 17.6 %shard_map.37 = bf16[256,4096]{1,0:T(8,128)(2,1)S(1)} custom-call(bf16[256,4096]{1,0:T(8,128)(2,1)S(1)} %copy-done, bf16[256,1024]{1,0:T(8,128)(2,1)S(1)} %copy-done.1, s32[1,85]{1,0:T(1,128)S(1)} %bitcast.1), custom_call_target="tpu_custom_call" | custom-call | flops 2013265920 | bytes 4718592 | tf_op jit(solution)/shard_map/pallas_call | solution.py:292
  20.9 1.3 %copy.5 = bf16[256,4096]{1,0:T(8,128)(2,1)} copy(bf16[256,4096]{1,0:T(8,128)(2,1)S(1)} %shard_map.37) | data formatting | bytes 4194304
Async XLA Ops:
  0.0 1.6 %copy-start = (bf16[256,4096]{1,0:T(8,128)(2,1)S(1)}, bf16[256,4096]{1,0:T(8,128)(2,1)}, u32[]{:S(2)}) copy-start(bf16[256,4096]{1,0:T(8,128)(2,1)} %proj.1) | copy-start | bytes 6291460
  1.6 1.0 %copy-start.1 = (bf16[256,1024]{1,0:T(8,128)(2,1)S(1)}, bf16[256,1024]{1,0:T(8,128)(2,1)}, u32[]{:S(2)}) copy-start(bf16[256,1024]{1,0:T(8,128)(2,1)} %grad.1) | copy-start | bytes 1572868
  2.6 0.7 %copy-start.2 = (s32[85]{0:T(128)S(1)}, s32[85]{0:T(128)}, u32[]{:S(2)}) copy-start(s32[85]{0:T(128)} %param.5) | copy-start | bytes 1024
where the time goes:
time: 22.6 us; the launch traced here: 22.2 us
  Pallas kernels  17.6 us (78%)
  local copies, waits for them, and re-layouts  4.61 us (20%)
    pallas_call x1, Pallas kernels, on_device(): pl.pallas_call(functools.partial(kernel, mesh.shape['dp'], mesh.shape['sh...  17.6 us
    unnamed x7, local copies, waits for them, and re-layouts  4.61 us

commit v1 on v0

--- a/solution.py
+++ b/solution.py
@@ -22,10 +22,10 @@
 
 def kernel(
     n_dp, n_shard,
-    proj, grad, lengths, out,
-    kv, q, u, dy, mixed, gm, weights, slopes, acc, ones, sixteenths, masks, result,
+    proj, grad, counts, result,
+    lengths, kv, q, u, dy, mixed, gm, weights, slopes, acc, ones, sixteenths, masks,
     outgoing, returned,
-    load_sem, store_sem, halo_send, halo_recv, back_send, back_recv,
+    load_sem, halo_send, halo_recv, back_send, back_recv,
 ):
     rows, width = q.shape
     quad = QUAD * (width // HEADS)
@@ -38,6 +38,9 @@
     last = n_dp * n_shard - 1
     has_prev, has_next = me > 0, me < last
 
+    def columns(c, part=0):
+        return pl.ds(part * width + c * quad, quad)
+
     def device(index):
         return {"dp": index // n_shard, "shard": index % n_shard}
 
@@ -61,22 +64,27 @@
         load(1, proj.at[:, pl.ds(0, width)], q),
         load(2, proj.at[:, pl.ds(3 * width, width)], u),
         load(3, grad, dy),
+        load(4, counts, lengths),
     ]
 
     pl.semaphore_wait(barrier, jnp.where(has_prev, 1, 0) + jnp.where(has_next, 1, 0))
 
-    halo = pltpu.make_async_remote_copy(
-        src_ref=proj.at[pl.ds(tail, MAXLEN), pl.ds(width, 2 * width)],
-        dst_ref=kv.at[pl.ds(0, MAXLEN), :],
-        send_sem=halo_send,
-        recv_sem=halo_recv,
-        device_id=device(jnp.where(has_next, me + 1, me - 1)),
-        device_id_type=MESH,
-    )
+    def halo(c, part):
+        return pltpu.make_async_remote_copy(
+            src_ref=proj.at[pl.ds(tail, MAXLEN), columns(c, 1 + part)],
+            dst_ref=kv.at[pl.ds(0, MAXLEN), columns(c, part)],
+            send_sem=halo_send.at[c, part],
+            recv_sem=halo_recv.at[c, part],
+            device_id=device(jnp.where(has_next, me + 1, me - 1)),
+            device_id_type=MESH,
+        )
+
+    halves = [(c, part) for c in range(quads) for part in range(2)]
 
     @pl.when(has_next)
     def _():
-        halo.start()
+        for c, part in halves:
+            halo(c, part).start()
 
     @pl.when(jnp.logical_not(has_prev))
     def _():
@@ -95,6 +103,8 @@
             device_id=device(jnp.where(has_prev, me - 1, me + 1)),
             device_id_type=MESH,
         )
+
+    loads[4].wait()
 
     base = (me * rows).astype(jnp.float32)
     lane = (lax.broadcasted_iota(jnp.int32, (1, quad), 1) % BLOCK).astype(jnp.float32)
@@ -133,9 +143,6 @@
     def block_rows(b):
         return pl.ds(b * BLOCK, BLOCK)
 
-    def columns(c, part=0):
-        return pl.ds(part * width + c * quad, quad)
-
     def per_head(transposed, values):
         halves = []
         for p in range(2):
@@ -207,38 +214,32 @@
         grad_q = per_head(grad_scores, keys) * 0.0625
         result[block_rows(b), columns(c)] = grad_q.astype(result.dtype)
 
-    stores = []
-
-    def store(row, height, column, span):
-        at = (pl.ds(row, height), pl.ds(column, span))
-        copy = pltpu.make_async_copy(result.at[at], out.at[at], store_sem.at[len(stores)])
-        copy.start()
-        stores.append(copy)
-
-    lower, upper = range(half), range(half, blocks)
-    split = half * BLOCK
+    lower, upper = range(blocks // 2), range(blocks // 2, blocks)
 
     for copy in loads[:2]:
         copy.wait()
     for c in range(quads):
         for b in upper:
             forward(b, c)
-    for copy in loads[2:]:
+    for copy in loads[2:4]:
         copy.wait()
     for b in upper:
         normalise(b)
-    store(split, rows - split, 3 * width, width)
-
-    @pl.when(has_prev)
-    def _():
-        halo.wait_recv()
-
-    for c in range(quads):
+    for c in range(quads):
+        for b in upper:
+            backward(b, c)
+
+    for c in range(quads):
+
+        @pl.when(has_prev)
+        def _():
+            halo(c, 0).wait_recv()
+            halo(c, 1).wait_recv()
+
         for b in lower:
             forward(b, c)
     for b in lower:
         normalise(b)
-    store(0, split, 3 * width, width)
     for c in range(quads):
         for b in lower:
             backward(b, c)
@@ -246,13 +247,6 @@
         @pl.when(has_prev)
         def _():
             backs(c).start()
-
-    store(0, split, 0, width)
-    for c in range(quads):
-        for b in upper:
-            backward(b, c)
-    store(split, rows - split, 0, width)
-    store(0, tail, width, 2 * width)
 
     for c in range(quads):
 
@@ -265,20 +259,16 @@
                 c, :, pl.ds(part * quad, quad)
             ].astype(jnp.float32)
             result[pl.ds(tail, MAXLEN), columns(c, 1 + part)] = total.astype(result.dtype)
-    store(tail, MAXLEN, width, 2 * width)
 
     @pl.when(has_next)
     def _():
-        halo.wait_send()
-
-    for c in range(quads):
-
-        @pl.when(has_prev)
-        def _():
+        for c, part in halves:
+            halo(c, part).wait_send()
+
+    @pl.when(has_prev)
+    def _():
+        for c in range(quads):
             backs(c).wait_send()
-
-    for copy in stores:
-        copy.wait()
 
 
 def on_device(mesh, projected, grad_gated, lengths):
@@ -288,13 +278,15 @@
     blocks = rows // BLOCK
     bf16, f32 = jnp.bfloat16, jnp.float32
     window = rows + MAXLEN
-    anywhere = pl.BlockSpec(memory_space=pl.ANY)
+    hbm = pl.BlockSpec(memory_space=pltpu.HBM)
+    counts = lengths.reshape(1, -1)
     return pl.pallas_call(
         functools.partial(kernel, mesh.shape["dp"], mesh.shape["shard"]),
         out_shape=jax.ShapeDtypeStruct((rows, 4 * width), bf16),
-        in_specs=[anywhere, anywhere, pl.BlockSpec(memory_space=pltpu.VMEM)],
-        out_specs=anywhere,
+        in_specs=[hbm, hbm, hbm],
+        out_specs=pl.BlockSpec(memory_space=pltpu.VMEM),
         scratch_shapes=[
+            pltpu.VMEM(counts.shape, jnp.int32),
             pltpu.VMEM((window, 2 * width), bf16),
             pltpu.VMEM((rows, width), bf16),
             pltpu.VMEM((rows, width), bf16),
@@ -307,13 +299,11 @@
             pltpu.VMEM((quad, quad), bf16),
             pltpu.VMEM((quad, quad), bf16),
             pltpu.VMEM((blocks, KEYS, quad), f32),
-            pltpu.VMEM((rows, 4 * width), bf16),
             pltpu.VMEM((quads, MAXLEN, 2 * quad), bf16),
             pltpu.VMEM((quads, MAXLEN, 2 * quad), bf16),
-            pltpu.SemaphoreType.DMA((4,)),
-            pltpu.SemaphoreType.DMA((6,)),
-            pltpu.SemaphoreType.DMA,
-            pltpu.SemaphoreType.DMA,
+            pltpu.SemaphoreType.DMA((5,)),
+            pltpu.SemaphoreType.DMA((quads, 2)),
+            pltpu.SemaphoreType.DMA((quads, 2)),
             pltpu.SemaphoreType.DMA((quads,)),
             pltpu.SemaphoreType.DMA((quads,)),
         ],
@@ -325,7 +315,7 @@
             bytes_accessed=rows * width * 2 * 9,
             transcendentals=rows * KEYS * HEADS,
         ),
-    )(projected, grad_gated, lengths.reshape(1, -1))
+    )(*(pltpu.with_memory_space_constraint(a, pltpu.HBM) for a in (projected, grad_gated, counts)))
 
 
 def solution(mesh):

time: 22.6 us -> 19.1 us (0.85)
  local copies, waits for them, and re-layouts: 4.61 us -> 1.32 us
    unnamed x7 -> x1, local copies, waits for them, and re-layouts: 4.61 us -> 1.32 us
where the time goes in v1:
time: 19.1 us; the launch traced here: 18.8 us
  Pallas kernels  17.5 us (92%)
  local copies, waits for them, and re-layouts  1.32 us (7%)
    pallas_call x1, Pallas kernels, on_device(): pl.pallas_call(functools.partial(kernel, mesh.shape['dp'], mesh.shape['sh...  17.5 us
    unnamed x1, local copies, waits for them, and re-layouts  1.32 us

profile of v1, /device:TPU:1, one launch (start us, length us, event | category | flops | bytes accessed | tf_op | source)
XLA Modules:
  0.0 18.8 jit_solution(13995945478806089601)
XLA Ops:
  0.0 17.5 %shard_map.37 = bf16[256,4096]{1,0:T(8,128)(2,1)S(1)} custom-call(bf16[256,4096]{1,0:T(8,128)(2,1)} %proj.1, bf16[256,1024]{1,0:T(8,128)(2,1)} %grad.1, s32[1,85]{1,0:T(1,128)} %bitcast.1), custom_call_target="tpu_custom_call" | custom-call | flops 2013265920 | bytes 4718592 | tf_op jit(solution)/shard_map/pallas_call | solution.py:283
  17.5 1.3 %copy.5 = bf16[256,4096]{1,0:T(8,128)(2,1)} copy(bf16[256,4096]{1,0:T(8,128)(2,1)S(1)} %shard_map.37) | data formatting | bytes 4194304

commit v2 on v1

--- a/solution.py
+++ b/solution.py
@@ -24,15 +24,14 @@
     n_dp, n_shard,
     proj, grad, counts, result,
     lengths, kv, q, u, dy, mixed, gm, weights, slopes, acc, ones, sixteenths, masks,
-    outgoing, returned,
     load_sem, halo_send, halo_recv, back_send, back_recv,
 ):
-    rows, width = q.shape
+    rows, width = dy.shape
     quad = QUAD * (width // HEADS)
     quads = width // quad
     blocks = rows // BLOCK
     tail = rows - MAXLEN
-    half = blocks // 2
+    every = q.shape[0] // BLOCK
 
     me = lax.axis_index("dp") * n_shard + lax.axis_index("shard")
     last = n_dp * n_shard - 1
@@ -61,7 +60,7 @@
 
     loads = [
         load(0, proj.at[:, pl.ds(width, 2 * width)], kv.at[pl.ds(MAXLEN, rows), :]),
-        load(1, proj.at[:, pl.ds(0, width)], q),
+        load(1, proj.at[:, pl.ds(0, width)], q.at[pl.ds(0, rows), :]),
         load(2, proj.at[:, pl.ds(3 * width, width)], u),
         load(3, grad, dy),
         load(4, counts, lengths),
@@ -92,24 +91,38 @@
 
     @pl.when(jnp.logical_not(has_next))
     def _():
-        returned[...] = jnp.zeros_like(returned)
-
-    def backs(c):
+        for ref in (q, gm):
+            ref[pl.ds(rows, MAXLEN), :] = jnp.zeros((MAXLEN, width), ref.dtype)
+
+    beyond = q.shape[0] - rows - MAXLEN
+    for ref in (q, gm):
+        ref[pl.ds(rows + MAXLEN, beyond), :] = jnp.zeros((beyond, width), ref.dtype)
+
+    def to_prev(i, source, target):
         return pltpu.make_async_remote_copy(
-            src_ref=outgoing.at[c],
-            dst_ref=returned.at[c],
-            send_sem=back_send.at[c],
-            recv_sem=back_recv.at[c],
+            src_ref=source,
+            dst_ref=target,
+            send_sem=back_send.at[i],
+            recv_sem=back_recv.at[i],
             device_id=device(jnp.where(has_prev, me - 1, me + 1)),
             device_id_type=MESH,
         )
 
+    def gm_part(i, row, height):
+        return to_prev(i, gm.at[pl.ds(row, height), :], gm.at[pl.ds(rows + row, height), :])
+
+    backs = [
+        to_prev(0, proj.at[pl.ds(0, MAXLEN), pl.ds(0, width)], q.at[pl.ds(rows, MAXLEN), :]),
+        gm_part(1, 0, BLOCK),
+        gm_part(2, BLOCK, MAXLEN - BLOCK),
+    ]
+
     loads[4].wait()
 
     base = (me * rows).astype(jnp.float32)
     lane = (lax.broadcasted_iota(jnp.int32, (1, quad), 1) % BLOCK).astype(jnp.float32)
-    positions = [base + float(b * BLOCK) + lane for b in range(blocks)]
-    starts = [jnp.zeros((1, quad), jnp.float32) for _ in range(blocks)]
+    positions = [base + float(b * BLOCK) + lane for b in range(every)]
+    starts = [jnp.zeros((1, quad), jnp.float32) for _ in range(every)]
     carry = jnp.zeros((1, 1), jnp.float32)
     count = lengths.shape[1]
     for first in range(0, count, 128):
@@ -120,11 +133,11 @@
         )
         ends = carry + jnp.sum(jnp.where(upto, part, 0.0), axis=1, keepdims=True)
         carry = carry + jnp.sum(part, axis=1, keepdims=True)
-        for b in range(blocks):
+        for b in range(every):
             reached = jnp.max(jnp.where(ends <= positions[b], ends, 0.0), axis=0, keepdims=True)
             starts[b] = jnp.maximum(starts[b], reached)
     offset = lax.broadcasted_iota(jnp.int32, (KEYS, quad), 0).astype(jnp.float32)
-    for b in range(blocks):
+    for b in range(every):
         key = offset + (base + float(b * BLOCK - MAXLEN))
         keep = (starts[b] <= key) & (key <= positions[b])
         masks[b] = jnp.where(keep, 1.0, 0.0)
@@ -151,17 +164,22 @@
             halves.append(jnp.where(left_head, both[:BLOCK], both[BLOCK:]))
         return jnp.concatenate(halves, 1)
 
+    def reach(b):
+        return min(KEYS, MAXLEN + rows - b * BLOCK)
+
     def forward(b, c):
-        keys = kv[pl.ds(b * BLOCK, KEYS), columns(c)]
-        values = kv[pl.ds(b * BLOCK, KEYS), columns(c, 1)]
+        span = reach(b)
+        keys = kv[pl.ds(b * BLOCK, span), columns(c)]
         queries = stacked(q[block_rows(b), columns(c)], sixteenths)
         h = dot(keys, queries, 1, 1)
         t = jnp.tanh(h)
-        kept = (1.0 + t) * masks[b]
+        kept = (1.0 + t) * masks[b, pl.ds(0, span), :]
         w = (h * kept).astype(weights.dtype)
-        weights[b, c] = w
-        slopes[b, c] = kept * (1.0 + h * (1.0 - t))
-        mixed[block_rows(b), columns(c)] = per_head(w, values)
+        weights[b, c, pl.ds(0, span), :] = w
+        slopes[b, c, pl.ds(0, span), :] = kept * (1.0 + h * (1.0 - t))
+        if b < blocks:
+            values = kv[pl.ds(b * BLOCK, span), columns(c, 1)]
+            mixed[block_rows(b), columns(c)] = per_head(w, values)
 
     def normalise(b):
         at = block_rows(b)
@@ -178,43 +196,45 @@
 
     written = set()
     left = {}
-    for e in range((MAXLEN + rows) // CHUNK):
-        users = [b for b in range(blocks) if b * BLOCK <= e * CHUNK < b * BLOCK + KEYS]
+    for e in range(MAXLEN // CHUNK, (MAXLEN + rows) // CHUNK):
+        users = [b for b in range(every) if b * BLOCK <= e * CHUNK < b * BLOCK + KEYS]
         for c in range(quads):
-            left[e, c] = len(users)
-
-    def add(b, c, part, value):
-        for i in range(KEYS // CHUNK):
-            e = b * BLOCK // CHUNK + i
+            for part in range(2):
+                left[e, c, part] = len(users)
+
+    def add(b, c, part, row, value):
+        for i in range(value.shape[0] // CHUNK):
+            key = (row // CHUNK + i, c, part)
             piece = value[i * CHUNK : (i + 1) * CHUNK]
-            at = pl.ds(e * CHUNK, CHUNK)
-            if (e, c, part) in written:
+            at = pl.ds(row + i * CHUNK, CHUNK)
+            if key in written:
                 piece = piece + acc[at, columns(c, part)]
-            written.add((e, c, part))
-            if part:
-                left[e, c] -= 1
-            remaining = left[e, c] if part else left[e, c] - 1
-            row = e * CHUNK - MAXLEN
-            if remaining or row >= tail:
+            written.add(key)
+            left[key] -= 1
+            if left[key]:
                 acc[at, columns(c, part)] = piece
-            elif row < 0:
-                outgoing[c, at, pl.ds(part * quad, quad)] = piece.astype(outgoing.dtype)
             else:
-                result[pl.ds(row, CHUNK), columns(c, 1 + part)] = piece.astype(result.dtype)
+                own = pl.ds(row + i * CHUNK - MAXLEN, CHUNK)
+                result[own, columns(c, 1 + part)] = piece.astype(result.dtype)
 
     def backward(b, c):
-        keys = kv[pl.ds(b * BLOCK, KEYS), columns(c)]
-        values = kv[pl.ds(b * BLOCK, KEYS), columns(c, 1)]
+        span = reach(b)
+        skip = max(0, MAXLEN - b * BLOCK)
+        keys = kv[pl.ds(b * BLOCK, span), columns(c)]
+        values = kv[pl.ds(b * BLOCK, span), columns(c, 1)]
         queries = stacked(q[block_rows(b), columns(c)], sixteenths)
         grads = stacked(gm[block_rows(b), columns(c)], ones)
         grad_weights = dot(values, grads, 1, 1)
-        grad_scores = (grad_weights * slopes[b, c]).astype(jnp.bfloat16)
-        add(b, c, 0, dot(grad_scores, queries, 1, 0))
-        add(b, c, 1, dot(weights[b, c], grads, 1, 0))
-        grad_q = per_head(grad_scores, keys) * 0.0625
-        result[block_rows(b), columns(c)] = grad_q.astype(result.dtype)
+        grad_scores = (grad_weights * slopes[b, c, pl.ds(0, span), :]).astype(jnp.bfloat16)
+        add(b, c, 0, b * BLOCK + skip, dot(grad_scores[skip:], queries, 1, 0))
+        w = weights[b, c, pl.ds(skip, span - skip), :]
+        add(b, c, 1, b * BLOCK + skip, dot(w, grads, 1, 0))
+        if b < blocks:
+            grad_q = per_head(grad_scores, keys) * 0.0625
+            result[block_rows(b), columns(c)] = grad_q.astype(result.dtype)
 
     lower, upper = range(blocks // 2), range(blocks // 2, blocks)
+    after = range(blocks, every)
 
     for copy in loads[:2]:
         copy.wait()
@@ -229,6 +249,10 @@
         for b in upper:
             backward(b, c)
 
+    @pl.when(has_prev)
+    def _():
+        backs[0].start()
+
     for c in range(quads):
 
         @pl.when(has_prev)
@@ -240,25 +264,31 @@
             forward(b, c)
     for b in lower:
         normalise(b)
+
+        @pl.when(has_prev)
+        def _():
+            backs[1 + b].start()
+
     for c in range(quads):
         for b in lower:
             backward(b, c)
 
-        @pl.when(has_prev)
-        def _():
-            backs(c).start()
-
-    for c in range(quads):
-
-        @pl.when(has_next)
-        def _():
-            backs(c).wait_recv()
-
-        for part in range(2):
-            total = acc[pl.ds(rows, MAXLEN), columns(c, part)] + returned[
-                c, :, pl.ds(part * quad, quad)
-            ].astype(jnp.float32)
-            result[pl.ds(tail, MAXLEN), columns(c, 1 + part)] = total.astype(result.dtype)
+    @pl.when(has_next)
+    def _():
+        backs[0].wait_recv()
+
+    for c in range(quads):
+        for b in after:
+            forward(b, c)
+
+    @pl.when(has_next)
+    def _():
+        backs[1].wait_recv()
+        backs[2].wait_recv()
+
+    for c in range(quads):
+        for b in after:
+            backward(b, c)
 
     @pl.when(has_next)
     def _():
@@ -267,15 +297,15 @@
 
     @pl.when(has_prev)
     def _():
-        for c in range(quads):
-            backs(c).wait_send()
+        for back in backs:
+            back.wait_send()
 
 
 def on_device(mesh, projected, grad_gated, lengths):
     rows, width = grad_gated.shape
     quad = QUAD * (width // HEADS)
     quads = width // quad
-    blocks = rows // BLOCK
+    blocks = rows // BLOCK + 2
     bf16, f32 = jnp.bfloat16, jnp.float32
     window = rows + MAXLEN
     hbm = pl.BlockSpec(memory_space=pltpu.HBM)
@@ -288,24 +318,22 @@
         scratch_shapes=[
             pltpu.VMEM(counts.shape, jnp.int32),
             pltpu.VMEM((window, 2 * width), bf16),
-            pltpu.VMEM((rows, width), bf16),
+            pltpu.VMEM((blocks * BLOCK, width), bf16),
             pltpu.VMEM((rows, width), bf16),
             pltpu.VMEM((rows, width), bf16),
             pltpu.VMEM((rows, width), f32),
-            pltpu.VMEM((rows, width), bf16),
+            pltpu.VMEM((blocks * BLOCK, width), bf16),
             pltpu.VMEM((blocks, quads, KEYS, quad), bf16),
             pltpu.VMEM((blocks, quads, KEYS, quad), f32),
             pltpu.VMEM((window, 2 * width), f32),
             pltpu.VMEM((quad, quad), bf16),
             pltpu.VMEM((quad, quad), bf16),
             pltpu.VMEM((blocks, KEYS, quad), f32),
-            pltpu.VMEM((quads, MAXLEN, 2 * quad), bf16),
-            pltpu.VMEM((quads, MAXLEN, 2 * quad), bf16),
             pltpu.SemaphoreType.DMA((5,)),
             pltpu.SemaphoreType.DMA((quads, 2)),
             pltpu.SemaphoreType.DMA((quads, 2)),
-            pltpu.SemaphoreType.DMA((quads,)),
-            pltpu.SemaphoreType.DMA((quads,)),
+            pltpu.SemaphoreType.DMA((3,)),
+            pltpu.SemaphoreType.DMA((3,)),
         ],
         compiler_params=pltpu.CompilerParams(
             collective_id=0, has_side_effects=True, vmem_limit_bytes=40 * 1024 * 1024

time: 19.1 us -> 17.1 us (0.90)
  Pallas kernels: 17.5 us -> 15.5 us
    pallas_call x1, Pallas kernels: 17.5 us -> 15.5 us  [on_device(): pl.pallas_call(functools.partial(kernel, mesh.shape['dp'], mesh.shape['sh...]
where the time goes in v2:
time: 17.1 us; the launch traced here: 16.8 us
  Pallas kernels  15.5 us (91%)
  local copies, waits for them, and re-layouts  1.32 us (8%)
    pallas_call x1, Pallas kernels, on_device(): pl.pallas_call(functools.partial(kernel, mesh.shape['dp'], mesh.shape['sh...  15.5 us
    unnamed x1, local copies, waits for them, and re-layouts  1.32 us

profile of v2, /device:TPU:1, one launch (start us, length us, event | category | flops | bytes accessed | tf_op | source)
XLA Modules:
  0.0 16.8 jit_solution(12660746635203062051)
XLA Ops:
  0.0 15.5 %shard_map.37 = bf16[256,4096]{1,0:T(8,128)(2,1)S(1)} custom-call(bf16[256,4096]{1,0:T(8,128)(2,1)} %proj.1, bf16[256,1024]{1,0:T(8,128)(2,1)} %grad.1, s32[1,85]{1,0:T(1,128)} %bitcast.1), custom_call_target="tpu_custom_call" | custom-call | flops 2013265920 | bytes 4718592 | tf_op jit(solution)/shard_map/pallas_call | solution.py:313
  15.5 1.3 %copy.5 = bf16[256,4096]{1,0:T(8,128)(2,1)} copy(bf16[256,4096]{1,0:T(8,128)(2,1)S(1)} %shard_map.37) | data formatting | bytes 4194304

commit v3 on v2

--- a/solution.py
+++ b/solution.py
@@ -68,22 +68,27 @@
 
     pl.semaphore_wait(barrier, jnp.where(has_prev, 1, 0) + jnp.where(has_next, 1, 0))
 
-    def halo(c, part):
+    def halo(i, row, height, column, span):
         return pltpu.make_async_remote_copy(
-            src_ref=proj.at[pl.ds(tail, MAXLEN), columns(c, 1 + part)],
-            dst_ref=kv.at[pl.ds(0, MAXLEN), columns(c, part)],
-            send_sem=halo_send.at[c, part],
-            recv_sem=halo_recv.at[c, part],
+            src_ref=proj.at[pl.ds(tail + row, height), pl.ds(width + column, span)],
+            dst_ref=kv.at[pl.ds(row, height), pl.ds(column, span)],
+            send_sem=halo_send.at[i],
+            recv_sem=halo_recv.at[i],
             device_id=device(jnp.where(has_next, me + 1, me - 1)),
             device_id_type=MESH,
         )
 
-    halves = [(c, part) for c in range(quads) for part in range(2)]
-
-    @pl.when(has_next)
-    def _():
-        for c, part in halves:
-            halo(c, part).start()
+    near = halo(0, BLOCK, MAXLEN - BLOCK, 0, 2 * width)
+    far = [
+        [halo(1 + 2 * c + part, 0, BLOCK, part * width + c * quad, quad) for part in range(2)]
+        for c in range(quads)
+    ]
+    halos = [near] + sum(far, [])
+
+    @pl.when(has_next)
+    def _():
+        for copy in halos:
+            copy.start()
 
     @pl.when(jnp.logical_not(has_prev))
     def _():
@@ -108,14 +113,18 @@
             device_id_type=MESH,
         )
 
-    def gm_part(i, row, height):
-        return to_prev(i, gm.at[pl.ds(row, height), :], gm.at[pl.ds(rows + row, height), :])
-
-    backs = [
-        to_prev(0, proj.at[pl.ds(0, MAXLEN), pl.ds(0, width)], q.at[pl.ds(rows, MAXLEN), :]),
-        gm_part(1, 0, BLOCK),
-        gm_part(2, BLOCK, MAXLEN - BLOCK),
-    ]
+    def gm_part(i, row, height, column, span):
+        lanes = pl.ds(column, span)
+        return to_prev(
+            i, gm.at[pl.ds(row, height), lanes], gm.at[pl.ds(rows + row, height), lanes]
+        )
+
+    back_q = to_prev(
+        0, proj.at[pl.ds(0, MAXLEN), pl.ds(0, width)], q.at[pl.ds(rows, MAXLEN), :]
+    )
+    back_second = gm_part(1, BLOCK, MAXLEN - BLOCK, 0, width)
+    back_first = [gm_part(2 + c, 0, BLOCK, c * quad, quad) for c in range(quads)]
+    backs = [back_q, back_second] + back_first
 
     loads[4].wait()
 
@@ -233,8 +242,7 @@
             grad_q = per_head(grad_scores, keys) * 0.0625
             result[block_rows(b), columns(c)] = grad_q.astype(result.dtype)
 
-    lower, upper = range(blocks // 2), range(blocks // 2, blocks)
-    after = range(blocks, every)
+    upper, after = range(2, blocks), range(blocks, every)
 
     for copy in loads[:2]:
         copy.wait()
@@ -251,31 +259,39 @@
 
     @pl.when(has_prev)
     def _():
-        backs[0].start()
+        back_q.start()
+        near.wait_recv()
+
+    for c in range(quads):
+        forward(1, c)
+    normalise(1)
+
+    @pl.when(has_prev)
+    def _():
+        back_second.start()
 
     for c in range(quads):
 
         @pl.when(has_prev)
         def _():
-            halo(c, 0).wait_recv()
-            halo(c, 1).wait_recv()
-
-        for b in lower:
-            forward(b, c)
-    for b in lower:
-        normalise(b)
-
-        @pl.when(has_prev)
-        def _():
-            backs[1 + b].start()
-
-    for c in range(quads):
-        for b in lower:
+            for copy in far[c]:
+                copy.wait_recv()
+
+        forward(0, c)
+    normalise(0)
+
+    @pl.when(has_prev)
+    def _():
+        for copy in back_first:
+            copy.start()
+
+    for b in (1, 0):
+        for c in range(quads):
             backward(b, c)
 
     @pl.when(has_next)
     def _():
-        backs[0].wait_recv()
+        back_q.wait_recv()
 
     for c in range(quads):
         for b in after:
@@ -283,22 +299,28 @@
 
     @pl.when(has_next)
     def _():
-        backs[1].wait_recv()
-        backs[2].wait_recv()
-
-    for c in range(quads):
-        for b in after:
-            backward(b, c)
-
-    @pl.when(has_next)
-    def _():
-        for c, part in halves:
-            halo(c, part).wait_send()
-
-    @pl.when(has_prev)
-    def _():
-        for back in backs:
-            back.wait_send()
+        back_second.wait_recv()
+
+    for c in range(quads):
+        backward(blocks + 1, c)
+
+    for c in range(quads):
+
+        @pl.when(has_next)
+        def _():
+            back_first[c].wait_recv()
+
+        backward(blocks, c)
+
+    @pl.when(has_next)
+    def _():
+        for copy in halos:
+            copy.wait_send()
+
+    @pl.when(has_prev)
+    def _():
+        for copy in backs:
+            copy.wait_send()
 
 
 def on_device(mesh, projected, grad_gated, lengths):
@@ -330,10 +352,10 @@
             pltpu.VMEM((quad, quad), bf16),
             pltpu.VMEM((blocks, KEYS, quad), f32),
             pltpu.SemaphoreType.DMA((5,)),
-            pltpu.SemaphoreType.DMA((quads, 2)),
-            pltpu.SemaphoreType.DMA((quads, 2)),
-            pltpu.SemaphoreType.DMA((3,)),
-            pltpu.SemaphoreType.DMA((3,)),
+            pltpu.SemaphoreType.DMA((1 + 2 * quads,)),
+            pltpu.SemaphoreType.DMA((1 + 2 * quads,)),
+            pltpu.SemaphoreType.DMA((2 + quads,)),
+            pltpu.SemaphoreType.DMA((2 + quads,)),
         ],
         compiler_params=pltpu.CompilerParams(
             collective_id=0, has_side_effects=True, vmem_limit_bytes=40 * 1024 * 1024

time: 17.1 us -> 16.1 us (0.942)
  Pallas kernels: 15.5 us -> 14.6 us
    pallas_call x1, Pallas kernels: 15.5 us -> 14.6 us  [on_device(): pl.pallas_call(functools.partial(kernel, mesh.shape['dp'], mesh.shape['sh...]
where the time goes in v3:
time: 16.1 us; the launch traced here: 15.9 us
  Pallas kernels  14.6 us (91%)
  local copies, waits for them, and re-layouts  1.32 us (8%)
    pallas_call x1, Pallas kernels, on_device(): pl.pallas_call(functools.partial(kernel, mesh.shape['dp'], mesh.shape['sh...  14.6 us
    unnamed x1, local copies, waits for them, and re-layouts  1.32 us

profile of v3, /device:TPU:1, one launch (start us, length us, event | category | flops | bytes accessed | tf_op | source)
XLA Modules:
  0.0 15.9 jit_solution(1954127815538196975)
XLA Ops:
  0.0 14.6 %shard_map.37 = bf16[256,4096]{1,0:T(8,128)(2,1)S(1)} custom-call(bf16[256,4096]{1,0:T(8,128)(2,1)} %proj.1, bf16[256,1024]{1,0:T(8,128)(2,1)} %grad.1, s32[1,85]{1,0:T(1,128)} %bitcast.1), custom_call_target="tpu_custom_call" | custom-call | flops 2013265920 | bytes 4718592 | tf_op jit(solution)/shard_map/pallas_call | solution.py:335
  14.6 1.3 %copy.5 = bf16[256,4096]{1,0:T(8,128)(2,1)} copy(bf16[256,4096]{1,0:T(8,128)(2,1)S(1)} %shard_map.37) | data formatting | bytes 4194304

commit v4 on v3

--- a/solution.py
+++ b/solution.py
@@ -12,6 +12,7 @@
 BLOCK = 64
 KEYS = BLOCK + MAXLEN
 QUAD = 4
+PIECES = 2
 CHUNK = 32
 MESH = pl.DeviceIdType.MESH
 
@@ -29,6 +30,7 @@
     rows, width = dy.shape
     quad = QUAD * (width // HEADS)
     quads = width // quad
+    piece_width = width // PIECES
     blocks = rows // BLOCK
     tail = rows - MAXLEN
     every = q.shape[0] // BLOCK
@@ -80,8 +82,11 @@
 
     near = halo(0, BLOCK, MAXLEN - BLOCK, 0, 2 * width)
     far = [
-        [halo(1 + 2 * c + part, 0, BLOCK, part * width + c * quad, quad) for part in range(2)]
-        for c in range(quads)
+        [
+            halo(1 + 2 * i + part, 0, BLOCK, part * width + i * piece_width, piece_width)
+            for part in range(2)
+        ]
+        for i in range(PIECES)
     ]
     halos = [near] + sum(far, [])
 
@@ -123,7 +128,9 @@
         0, proj.at[pl.ds(0, MAXLEN), pl.ds(0, width)], q.at[pl.ds(rows, MAXLEN), :]
     )
     back_second = gm_part(1, BLOCK, MAXLEN - BLOCK, 0, width)
-    back_first = [gm_part(2 + c, 0, BLOCK, c * quad, quad) for c in range(quads)]
+    back_first = [
+        gm_part(2 + i, 0, BLOCK, i * piece_width, piece_width) for i in range(PIECES)
+    ]
     backs = [back_q, back_second] + back_first
 
     loads[4].wait()
@@ -157,7 +164,8 @@
     )
     ones[...] = jnp.where(own_head, 1.0, 0.0).astype(ones.dtype)
     sixteenths[...] = jnp.where(own_head, 0.0625, 0.0).astype(ones.dtype)
-    left_head = lax.broadcasted_iota(jnp.int32, (BLOCK, quad // 2), 1) < quad // QUAD
+    head = quad // QUAD
+    left_head = lax.broadcasted_iota(jnp.int32, (BLOCK, 2 * head), 1) < head
 
     def stacked(value, head_mask):
         return jnp.concatenate([value] * QUAD, 0) * head_mask[...]
@@ -166,12 +174,13 @@
         return pl.ds(b * BLOCK, BLOCK)
 
     def per_head(transposed, values):
-        halves = []
-        for p in range(2):
-            lanes = slice(p * quad // 2, (p + 1) * quad // 2)
-            both = dot(transposed[:, lanes], values[:, lanes], 0, 0)
-            halves.append(jnp.where(left_head, both[:BLOCK], both[BLOCK:]))
-        return jnp.concatenate(halves, 1)
+        pairs = []
+        for p in range(QUAD // 2):
+            stack = slice(p * 2 * BLOCK, (p + 1) * 2 * BLOCK)
+            lanes = slice(p * 2 * head, (p + 1) * 2 * head)
+            both = dot(transposed[:, stack], values[:, lanes], 0, 0)
+            pairs.append(jnp.where(left_head, both[:BLOCK], both[BLOCK:]))
+        return jnp.concatenate(pairs, 1)
 
     def reach(b):
         return min(KEYS, MAXLEN + rows - b * BLOCK)
@@ -242,6 +251,9 @@
             grad_q = per_head(grad_scores, keys) * 0.0625
             result[block_rows(b), columns(c)] = grad_q.astype(result.dtype)
 
+    def piece(i):
+        return range(i * quads // PIECES, (i + 1) * quads // PIECES)
+
     upper, after = range(2, blocks), range(blocks, every)
 
     for copy in loads[:2]:
@@ -270,14 +282,15 @@
     def _():
         back_second.start()
 
-    for c in range(quads):
+    for i in range(PIECES):
 
         @pl.when(has_prev)
         def _():
-            for copy in far[c]:
+            for copy in far[i]:
                 copy.wait_recv()
 
-        forward(0, c)
+        for c in piece(i):
+            forward(0, c)
     normalise(0)
 
     @pl.when(has_prev)
@@ -304,13 +317,14 @@
     for c in range(quads):
         backward(blocks + 1, c)
 
-    for c in range(quads):
+    for i in range(PIECES):
 
         @pl.when(has_next)
         def _():
-            back_first[c].wait_recv()
-
-        backward(blocks, c)
+            back_first[i].wait_recv()
+
+        for c in piece(i):
+            backward(blocks, c)
 
     @pl.when(has_next)
     def _():
@@ -352,10 +366,10 @@
             pltpu.VMEM((quad, quad), bf16),
             pltpu.VMEM((blocks, KEYS, quad), f32),
             pltpu.SemaphoreType.DMA((5,)),
-            pltpu.SemaphoreType.DMA((1 + 2 * quads,)),
-            pltpu.SemaphoreType.DMA((1 + 2 * quads,)),
-            pltpu.SemaphoreType.DMA((2 + quads,)),
-            pltpu.SemaphoreType.DMA((2 + quads,)),
+            pltpu.SemaphoreType.DMA((1 + 2 * PIECES,)),
+            pltpu.SemaphoreType.DMA((1 + 2 * PIECES,)),
+            pltpu.SemaphoreType.DMA((2 + PIECES,)),
+            pltpu.SemaphoreType.DMA((2 + PIECES,)),
         ],
         compiler_params=pltpu.CompilerParams(
             collective_id=0, has_side_effects=True, vmem_limit_bytes=40 * 1024 * 1024

time: 16.1 us -> 15.7 us (0.975)
  Pallas kernels: 14.6 us -> 14.1 us
    pallas_call x1, Pallas kernels: 14.6 us -> 14.1 us  [on_device(): pl.pallas_call(functools.partial(kernel, mesh.shape['dp'], mesh.shape['sh...]
where the time goes in v4:
time: 15.7 us; the launch traced here: 15.4 us
  Pallas kernels  14.1 us (90%)
  local copies, waits for them, and re-layouts  1.32 us (8%)
    pallas_call x1, Pallas kernels, on_device(): pl.pallas_call(functools.partial(kernel, mesh.shape['dp'], mesh.shape['sh...  14.1 us
    unnamed x1, local copies, waits for them, and re-layouts  1.32 us

profile of v4, /device:TPU:1, one launch (start us, length us, event | category | flops | bytes accessed | tf_op | source)
XLA Modules:
  0.0 15.4 jit_solution(11840148816931606313)
XLA Ops:
  0.0 14.1 %shard_map.37 = bf16[256,4096]{1,0:T(8,128)(2,1)S(1)} custom-call(bf16[256,4096]{1,0:T(8,128)(2,1)} %proj.1, bf16[256,1024]{1,0:T(8,128)(2,1)} %grad.1, s32[1,85]{1,0:T(1,128)} %bitcast.1), custom_call_target="tpu_custom_call" | custom-call | flops 2013265920 | bytes 4718592 | tf_op jit(solution)/shard_map/pallas_call | solution.py:349
  14.1 1.3 %copy.5 = bf16[256,4096]{1,0:T(8,128)(2,1)} copy(bf16[256,4096]{1,0:T(8,128)(2,1)S(1)} %shard_map.37) | data formatting | bytes 4194304
